TPU v7x, 512 devices: a whole 4x4x16 slice. The times are simulated.
512 devices in a mesh: seq: 32 (over z, core), head: 4 (over x), dp: 4 (over y).
Axes of the slice: x: 4, y: 4, z: 16, core: 2. Of those that a mesh axis runs over, the one named last changes fastest.
Arguments:
- passthrough: bfloat16 [4, 8192, 1024], P('dp', 'seq', 'head'), may hold values from -6 to 6
- mixed_out: bfloat16 [4, 8192, 1024], P('dp', 'seq', 'head'), may hold values from -6 to 6
- grad_mixed: bfloat16 [4, 8192, 1024], P('dp', 'seq', 'head'), may hold values from -6 to 6
- grad_pass: bfloat16 [4, 8192, 1024], P('dp', 'seq', 'head'), may hold values from -6 to 6
- query_weight: bfloat16 [1024, 1024], P(None, 'head'), may hold values from -0.1875 to 0.1875
- key_weight: bfloat16 [1024, 1024], P(None, 'head'), may hold values from -0.1875 to 0.1875
- value_weight: bfloat16 [1024, 1024], P(None, 'head'), may hold values from -0.1875 to 0.1875
- random_features: bfloat16 [8, 128, 256], P('head'), may hold values from -5 to 5
- document_ids: int32 [4, 8192], P('dp', 'seq'), may hold values from 0 to 27, never falling along the last dimension, each value on 1 to 2048 neighbouring positions
Outputs:
- first_in: bfloat16 [4, 8192, 1024], P('dp', 'seq', 'head')
- grad_second: bfloat16 [4, 8192, 1024], P('dp', 'seq', 'head')
- grad_query_weight: float32 [1024, 1024], P(('seq', 'dp'), 'head')
- grad_key_weight: float32 [1024, 1024], P(('seq', 'dp'), 'head')
- grad_value_weight: float32 [1024, 1024], P(('seq', 'dp'), 'head')
Inputs may be any that keep to these rules, and one draw needn't show every extreme that they name: `document_ids`: along each context the number never falls; each of the 28 documents holds 1 to 2048 positions, and one holds exactly 2048.
All inputs are finite; a program needn't handle non-finite values.
Results may differ from a plain program's by a relative error of at most 0.018.
The roundings to bfloat16 on the way count: a program that leaves them out, or rounds other values in their place, can miss the bound.
Values may be sent and summed in bfloat16 or wider, within the bound.
A program may use at most 64 MiB of HBM per device.

v0:
```python
import jax
import jax.numpy as jnp
from jax import lax
from jax.sharding import PartitionSpec as P

EPSILON = 1e-06
HIGHEST = lax.Precision.HIGHEST


def carried_in(array, axis, join, neutral, backward):
    count = lax.axis_size(axis)
    place = lax.axis_index(axis)
    ahead = count - 1 - place if backward else place
    gathered = jax.tree.map(
        lambda a, kind: lax.all_gather(a.astype(kind), axis), array, (jnp.bfloat16, jnp.bfloat16)
    )
    state = jax.tree.map(lambda a, e: jnp.zeros_like(a) + jnp.asarray(e, a.dtype), array, neutral)

    def one(turn, state):
        source = count - 1 - turn if backward else turn
        return join(
            state,
            jax.tree.map(
                lambda a, own: lax.dynamic_index_in_dim(a, source, 0, False).astype(own.dtype),
                gathered,
                array,
            ),
        )

    return lax.fori_loop(0, ahead, one, state)


def to_heads(matrix, head_count):
    count_ctx, tok_rows, columns = matrix.shape
    return matrix.reshape(count_ctx, tok_rows, head_count, columns // head_count).transpose(
        0, 2, 1, 3
    )


def from_heads(tensor):
    count_ctx, head_count, tok_rows, head_dim = tensor.shape
    return tensor.transpose(0, 2, 1, 3).reshape(count_ctx, tok_rows, head_count * head_dim)


def feature_map(projected, random_features):
    head_dim = projected.shape[-1]
    mixing = jnp.einsum(
        "chtd,hdm->chtm", projected, random_features, preferred_element_type=jnp.float32
    )
    widened = projected.astype(jnp.float32)
    squares = jnp.sum(widened * widened, axis=-1, keepdims=True)
    exponent = mixing / head_dim**0.25 - squares / (2.0 * head_dim**0.5)
    return (jnp.exp(exponent) / random_features.shape[-1] ** 0.5).astype(jnp.bfloat16)


def feature_grad(dfeature, feature, projected, random_features):
    head_dim = projected.shape[-1]
    dexponent = dfeature * feature.astype(jnp.float32)
    rounded = dexponent.astype(jnp.bfloat16)
    back_proj = jnp.einsum(
        "chtm,hdm->chtd", rounded, random_features, preferred_element_type=jnp.float32
    )
    totals = jnp.sum(dexponent, axis=-1, keepdims=True)
    result = back_proj / head_dim**0.25 - projected.astype(jnp.float32) * totals / head_dim**0.5
    return result.astype(jnp.bfloat16)


def join_state(earlier, later_part):
    early_state, early_id = earlier
    late_state, late_id = later_part
    same_id = (early_id == late_id)[:, None, None, None]
    vacant = (late_id < 0.0)[:, None, None, None]
    merged = jnp.where(vacant, early_state, late_state + jnp.where(same_id, early_state, 0.0))
    new_id = jnp.where(late_id < 0.0, early_id, late_id)
    return (merged, new_id)


def shards(
    passthrough,
    mixed_out,
    grad_mixed,
    grad_pass,
    query_weight,
    key_weight,
    value_weight,
    random_features,
    document_ids,
):
    head_count = random_features.shape[0]
    count_ctx, tok_rows, local_width = passthrough.shape
    whole_in = lax.all_gather(passthrough, "head", axis=2, tiled=True)
    widened = whole_in.astype(jnp.float32)
    full_width = widened.shape[2]
    inv_rms = lax.rsqrt(jnp.mean(widened * widened, axis=2, keepdims=True) + EPSILON)
    normed = (widened * inv_rms).astype(jnp.bfloat16)
    query_proj = jnp.einsum(
        "ctd,dj->ctj", normed, query_weight, preferred_element_type=jnp.float32
    ).astype(jnp.bfloat16)
    key_proj = jnp.einsum(
        "ctd,dj->ctj", normed, key_weight, preferred_element_type=jnp.float32
    ).astype(jnp.bfloat16)
    value_proj = jnp.einsum(
        "ctd,dj->ctj", normed, value_weight, preferred_element_type=jnp.float32
    ).astype(jnp.bfloat16)
    query_heads = to_heads(query_proj, head_count)
    key_heads = to_heads(key_proj, head_count)
    value_heads = to_heads(value_proj, head_count)
    feat_query = feature_map(query_heads, random_features)
    feat_key = feature_map(key_heads, random_features)
    ids_wide = document_ids.astype(jnp.float32)
    rows_idx = lax.broadcasted_iota(jnp.int32, (tok_rows, tok_rows), 0)
    cols_idx = lax.broadcasted_iota(jnp.int32, (tok_rows, tok_rows), 1)
    same_doc = document_ids[:, :, None] == document_ids[:, None, :]
    allowed = (same_doc & (rows_idx >= cols_idx)[None])[:, None]
    scores = jnp.einsum("chtm,chsm->chts", feat_query, feat_key, preferred_element_type=jnp.float32)
    pair_weight = jnp.where(allowed, scores, 0.0).astype(jnp.bfloat16)
    attn_local = jnp.einsum(
        "chts,chsd->chtd", pair_weight, value_heads, preferred_element_type=jnp.float32
    )
    last_ids = ids_wide[:, -1]
    tail_mask = (ids_wide == last_ids[:, None])[:, None, :, None]
    tail_keys = jnp.where(tail_mask, feat_key, jnp.zeros_like(feat_key))
    tail_state = jnp.einsum(
        "chtm,chtd->chmd", tail_keys, value_heads, preferred_element_type=jnp.float32
    )
    empty_state = (jnp.zeros_like(tail_state), jnp.full_like(last_ids, -1.0))
    state_in, state_id = carried_in((tail_state, last_ids), "seq", join_state, empty_state, False)
    head_on = (ids_wide == state_id[:, None])[:, None, :, None]
    fq_wide = feat_query.astype(jnp.float32)
    carried = jnp.einsum("chtm,chmd->chtd", fq_wide, state_in, precision=HIGHEST)
    attention = attn_local + jnp.where(head_on, carried, 0.0)
    inv_attn = lax.rsqrt(jnp.mean(attention * attention, axis=-1, keepdims=True) + EPSILON)
    act = attention * inv_attn
    first_in = (mixed_out.astype(jnp.float32) - from_heads(act)).astype(jnp.bfloat16)
    grad_act = to_heads(grad_mixed, head_count).astype(jnp.float32)
    grad_attn = (
        inv_attn * (grad_act - act * jnp.mean(grad_act * act, axis=-1, keepdims=True))
    ).astype(jnp.bfloat16)
    dscores = jnp.einsum(
        "chtd,chsd->chts", grad_attn, value_heads, preferred_element_type=jnp.float32
    )
    dpair = jnp.where(allowed, dscores, 0.0).astype(jnp.bfloat16)
    first_ids = ids_wide[:, 0]
    head_mask = (ids_wide == first_ids[:, None])[:, None, :, None]
    head_query = jnp.where(head_mask, feat_query, jnp.zeros_like(feat_query))
    head_state = jnp.einsum(
        "chtm,chtd->chmd", head_query, grad_attn, preferred_element_type=jnp.float32
    )
    state_later, later_id = carried_in(
        (head_state, first_ids), "seq", join_state, empty_state, True
    )
    tail_on = (ids_wide == later_id[:, None])[:, None, :, None]
    grad_wide = grad_attn.astype(jnp.float32)
    dfeat_query = jnp.einsum("chts,chsm->chtm", dpair, feat_key, preferred_element_type=jnp.float32)
    dfeat_query = dfeat_query + jnp.where(
        head_on, jnp.einsum("chtd,chmd->chtm", grad_wide, state_in, precision=HIGHEST), 0.0
    )
    dfeat_key = jnp.einsum("chts,chtm->chsm", dpair, feat_query, preferred_element_type=jnp.float32)
    dfeat_key = dfeat_key + jnp.where(
        tail_on,
        jnp.einsum(
            "chsd,chmd->chsm", value_heads.astype(jnp.float32), state_later, precision=HIGHEST
        ),
        0.0,
    )
    dvalue = jnp.einsum(
        "chts,chtd->chsd", pair_weight, grad_attn, preferred_element_type=jnp.float32
    )
    dvalue = dvalue + jnp.where(
        tail_on,
        jnp.einsum("chsm,chmd->chsd", feat_key.astype(jnp.float32), state_later, precision=HIGHEST),
        0.0,
    )
    dvalue = dvalue.astype(jnp.bfloat16)
    dquery = feature_grad(dfeat_query, feat_query, query_heads, random_features)
    dkey = feature_grad(dfeat_key, feat_key, key_heads, random_features)
    grads_flat = jnp.concatenate([from_heads(dquery), from_heads(dkey), from_heads(dvalue)], axis=2)
    weights_all = jnp.concatenate([query_weight, key_weight, value_weight], axis=1)
    partial_value = jnp.einsum(
        "ctj,dj->ctd", grads_flat, weights_all, preferred_element_type=jnp.float32
    )
    grad_normed = lax.psum_scatter(
        partial_value.astype(jnp.bfloat16), "head", scatter_dimension=2, tiled=True
    ).astype(jnp.float32)
    norm_local = passthrough.astype(jnp.float32) * inv_rms
    dot_sum = lax.psum(jnp.sum(grad_normed * norm_local, axis=2), "head")
    grad_second = grad_pass.astype(jnp.float32) + inv_rms * (
        grad_normed - norm_local * (dot_sum / full_width)[:, :, None]
    )
    grad_second = grad_second.astype(jnp.bfloat16)
    seq_count = lax.axis_size("seq")
    dp_count = lax.axis_size("dp")
    total_rows = count_ctx * tok_rows * seq_count * dp_count
    grad_scale = 1.0 / total_rows**0.5
    summed = lax.psum_scatter(
        jnp.einsum("ctr,ctj->rj", normed, grads_flat, preferred_element_type=jnp.float32)
        * grad_scale,
        ("seq", "dp"),
        scatter_dimension=0,
        tiled=True,
    )
    return (
        first_in,
        grad_second,
        summed[:, :local_width],
        summed[:, local_width : 2 * local_width],
        summed[:, 2 * local_width :],
    )


def solution(mesh):
    placed = (
        P("dp", "seq", "head"),
        P("dp", "seq", "head"),
        P("dp", "seq", "head"),
        P("dp", "seq", "head"),
        P(None, "head"),
        P(None, "head"),
        P(None, "head"),
        P("head", None, None),
        P("dp", "seq"),
    )
    return jax.shard_map(
        shards,
        mesh=mesh,
        in_specs=placed,
        out_specs=(
            P("dp", "seq", "head"),
            P("dp", "seq", "head"),
            P(("seq", "dp"), "head"),
            P(("seq", "dp"), "head"),
            P(("seq", "dp"), "head"),
        ),
        check_vma=False,
    )
```

profile of v0, /device:TPU:1, one launch (start us, length us, event | category | flops | bytes accessed | tf_op | source)
XLA Modules:
  0.0 688.5 jit_solution(1416142091037650247)
XLA Ops:
  7.3 0.8 convert_element_type.194
  8.6 11.3 %all_gather.23 = bf16[1,256,1024]{2,1,0:T(8,128)(2,1)S(1)} all-gather(bf16[1,256,256]{2,1,0:T(8,128)(2,1)} %param.13), channel_id=1, replica_groups=mesh['seq'=32,'head'=4,'dp'=4] {'head'}, dimensions={2}, use_global_device_ids=true | all-gather | bytes 655360 | tf_op jit(solution)/shard_map/all_gather | solution.py:91
  20.1 1.5 convolution_convert_fusion.3
  21.6 1.5 convolution_convert_fusion.2
  23.2 1.3 compare_reduce_fusion.1
  24.9 0.9 convolution_convert_fusion.1
  27.2 1.3 dynamic-slice
  28.5 0.7 dynamic-update-slice.1
  29.3 0.7 dynamic-update-slice
  30.0 56.4 %all-reduce.2 = (bf16[32]{0:T(256)(128)(2,1)S(1)}, bf16[32]{0:T(256)(128)(2,1)S(1)}) all-reduce(bf16[32]{0:T(256)(128)(2,1)S(1)} %dynamic-update-slice, bf16[32]{0:T(256)(128)(2,1)S(1)} %dynamic-update-slice.1), channel_id=1, replica_groups=mesh['seq'=32,'head'=4,'dp'=4] {'seq'}, use_global_device_ids=true, to_apply=%add | all-reduce | flops 64 | bytes 256
  87.6 20.5 %all-gather.5.cloned.1.call-done = bf16[64,256,128]{2,1,0:T(8,128)(2,1)} async-done(((bf16[2,256,128]{2,1,0:T(8,128)(2,1)}), bf16[64,256,128]{2,1,0:T(8,128)(2,1)}) %all-gather.5.cloned.1.call-update) | async-done | bytes 4194320 | tf_op jit(solution)/shard_map/all_gather | solution.py:15
  108.1 3.6 while.26
  110.7 1.0 fusion.110
  112.5 0.9 convolution_convert_fusion
  115.1 173.1 %all-gather.7.cloned.1.call-done = bf16[64,256,128]{2,1,0:T(8,128)(2,1)} async-done(((bf16[2,256,128]{2,1,0:T(8,128)(2,1)}), bf16[64,256,128]{2,1,0:T(8,128)(2,1)}) %all-gather.7.cloned.1.call-update) | async-done | bytes 4194320 | tf_op jit(solution)/shard_map/all_gather | solution.py:15
  288.2 108.2 %while.27 = (s32[]{:T(128)}, f32[1,2,256,128]{3,2,1,0:T(8,128)S(1)}, f32[1]{0:T(128)}, s32[]{:T(128)}, bf16[32,1]{0,1:T(2,128)(2,1)S(1)}, /*index=5*/bf16[32,1,2...) while((s32[]{:T(128)}, ...), condition=%wide.region_9.10_spmd, body=%wide.region_8.9_spmd.sunk | while | flops 262153 | bytes 655570 | solution.py:30
  288.2 0.6 constant_dynamic-slice_fusion.5
  290.7 1.0 fusion.111
  291.8 0.6 constant_dynamic-slice_fusion.5
  294.4 1.0 fusion.111
  295.4 0.6 constant_dynamic-slice_fusion.5
  298.0 1.0 fusion.111
  299.0 0.6 constant_dynamic-slice_fusion.5
  301.6 1.0 fusion.111
  302.6 0.6 constant_dynamic-slice_fusion.5
  305.2 1.0 fusion.111
  306.2 0.6 constant_dynamic-slice_fusion.5
  308.8 1.0 fusion.111
  309.8 0.6 constant_dynamic-slice_fusion.5
  312.4 1.0 fusion.111
  313.5 0.6 constant_dynamic-slice_fusion.5
  316.0 1.0 fusion.111
  319.6 1.0 fusion.111
  323.2 1.0 fusion.111
  326.8 1.0 fusion.111
  330.4 1.0 fusion.111
  334.0 1.0 fusion.111
  337.6 1.0 fusion.111
  341.3 1.0 fusion.111
  344.9 1.0 fusion.111
  348.5 1.0 fusion.111
  352.1 1.0 fusion.111
  355.7 1.0 fusion.111
  359.3 1.0 fusion.111
  362.9 1.0 fusion.111
  366.5 1.0 fusion.111
  367.6 0.6 constant_dynamic-slice_fusion.5
  370.1 1.0 fusion.111
  373.7 1.0 fusion.111
  377.3 1.0 fusion.111
  380.9 1.0 fusion.111
  384.5 1.0 fusion.111
  388.1 1.0 fusion.111
  391.8 1.0 fusion.111
  395.4 1.0 fusion.111
  397.5 2.8 fusion.11
  400.4 2.4 convolution_multiply_fusion
  403.0 0.7 subtract_convert_fusion
  403.7 18.7 %reduce-scatter.3.cloned.1.call-done = bf16[1,256,256]{2,1,0:T(8,128)(2,1)} async-done(((bf16[1,256,1024]{2,1,0:T(8,128)(2,1)}), bf16[1,256,256]{2,1,0:T(8,128)(2,1)}) %reduce-scatter.3.cloned.1.call-update) | async-done | bytes 131088 | tf_op jit(solution)/shard_map/reduce_scatter | solution.py:182
  422.4 1.1 fusion.43
  423.5 6.1 psum.7
  429.7 1.7 fusion.46
  431.4 249.3 %reduce-scatter.5.cloned.1.call-done = f32[8,768]{1,0:T(8,128)} async-done(((f32[1024,768]{1,0:T(8,128)}), f32[8,768]{1,0:T(8,128)}) %reduce-scatter.5.cloned.1.call-update) | async-done | bytes 24592 | tf_op jit(solution)/shard_map/reduce_scatter | solution.py:195
  680.7 1.3 fusion.85
  (81 shorter events, 19.3 us)
Async XLA Ops:
  7.2 17.4 %copy-start = (bf16[2,128,256]{2,1,0:T(8,128)(2,1)S(1)}, bf16[2,128,256]{2,1,0:T(8,128)(2,1)}, u32[]{:S(2)}) copy-start(bf16[2,128,256]{2,1,0:T(8,128)(2,1)} %param.20) | copy-start | bytes 393220
  7.2 16.0 %copy-start.5 = (s32[1,256]{1,0:T(1,128)S(1)}, s32[1,256]{1,0:T(1,128)}, u32[]{:S(2)}) copy-start(s32[1,256]{1,0:T(1,128)} %param.21) | copy-start | bytes 3076
  7.2 19.9 %copy-start.2 = (bf16[1,256,256]{2,1,0:T(8,128)(2,1)S(1)}, bf16[1,256,256]{2,1,0:T(8,128)(2,1)}, u32[]{:S(2)}) copy-start(bf16[1,256,256]{2,1,0:T(8,128)(2,1)} %param.15) | copy-start | bytes 393220
  7.2 79.2 %copy-start.6 = (bf16[1024,256]{1,0:T(8,128)(2,1)S(1)}, bf16[1024,256]{1,0:T(8,128)(2,1)}, u32[]{:S(2)}) copy-start(bf16[1024,256]{1,0:T(8,128)(2,1)} %param.17) | copy-start | bytes 1572868
  7.2 100.9 %all-gather.5.cloned.1.call-start = ((), (), s32[]{:S(2)}) async-start(), calls=%async_computation.4 | async-start | bytes 4325376 | tf_op jit(solution)/shard_map/all_gather | solution.py:15
  25.8 262.4 %all-gather.7.cloned.1.call-start = ((), (), s32[]{:S(2)}) async-start(), calls=%async_computation.5 | async-start | bytes 4325376 | tf_op jit(solution)/shard_map/all_gather | solution.py:15
  113.4 309.0 %reduce-scatter.3.cloned.1.call-start = ((), (), s32[]{:S(2)}) async-start(), calls=%async_computation.2 | async-start | bytes 655360 | tf_op jit(solution)/shard_map/reduce_scatter | solution.py:182
  400.3 2.7 copy-start.3
  400.4 22.1 %copy-start.1 = (bf16[1,256,256]{2,1,0:T(8,128)(2,1)S(1)}, bf16[1,256,256]{2,1,0:T(8,128)(2,1)}, u32[]{:S(2)}) copy-start(bf16[1,256,256]{2,1,0:T(8,128)(2,1)} %param.13) | copy-start | bytes 393220
  400.4 280.3 %reduce-scatter.5.cloned.1.call-start = ((), (), s32[]{:S(2)}) async-start(), calls=%async_computation.3 | async-start | bytes 3170304 | tf_op jit(solution)/shard_map/reduce_scatter | solution.py:195
  402.8 26.8 %copy-start.4 = (bf16[1,256,256]{2,1,0:T(8,128)(2,1)S(1)}, bf16[1,256,256]{2,1,0:T(8,128)(2,1)}, u32[]{:S(2)}) copy-start(bf16[1,256,256]{2,1,0:T(8,128)(2,1)} %param.16) | copy-start | bytes 393220
Sparse Core Ops, SparseCore 0:
  25.9 82.1 all-gather.4
  113.6 174.5 all-gather.6
  400.5 21.9 reduce-scatter.2
  427.0 253.6 reduce-scatter.4
where the time goes:
time: 701 us; the launch traced here: 689 us
  waiting for transfers between devices  462 us (66%)
  blocking collectives  73.8 us (11%)
  loops' own time  61.4 us (9%)
  other arithmetic  38.4 us (5%)
  local copies, waits for them, and re-layouts  23.3 us (3%)
  between operations  15.4 us (2%)
  matrix products  14.5 us (2%)
    reduce_scatter x1, waiting for transfers between devices, shards(): lax.psum_scatter(jnp.einsum('ctr,ctj->rj', normed, grads_flat, preferred_...  249 us
    all_gather x2, waiting for transfers between devices, carried_in(): lax.all_gather(a.astype(kind), axis)  194 us
    another operation x2, loops' own time, carried_in(): return lax.fori_loop(0, ahead, one, state)  61.4 us
    unnamed x1, blocking collectives  56.4 us
    select_n x31, other arithmetic, join_state(): jnp.where(vacant, early_state, late_state + jnp.where(same_id, early_stat...  32.2 us
    reduce_scatter x1, waiting for transfers between devices, shards(): lax.psum_scatter(partial_value.astype(jnp.bfloat16), 'head', scatter_dime...  18.7 us
    dynamic_slice x31, local copies, waits for them, and re-layouts, one(): lax.dynamic_index_in_dim(a, source, 0, False).astype(own.dtype)  18.2 us
  transfers between devices with their start and end apart: 4, of which 4 were waited for; matrix products, arithmetic and copies ran while one was open for 2% of the time, Pallas kernels for 0%

commit v1 on v0

v1 whole, which is shorter than its diff:
```python
import functools

import jax
import jax.numpy as jnp
from jax import lax
from jax.experimental import pallas as pl
from jax.experimental.pallas import tpu as pltpu
from jax.sharding import PartitionSpec as P

MESH = pl.DeviceIdType.MESH
BF = jnp.bfloat16
F32 = jnp.float32
EPSILON = 1e-06
TOK = 256
D = 1024
WID = 256
HD = 128
FEAT = 256
IDR = 16
MSG = FEAT + IDR
NX = 4


def nn(a, b):
    return jnp.dot(a, b, preferred_element_type=F32)


def nt(a, b):
    return lax.dot_general(a, b, (((1,), (1,)), ((), ())), preferred_element_type=F32)


def tn(a, b):
    return lax.dot_general(a, b, (((0,), (0,)), ((), ())), preferred_element_type=F32)


def kernel(
    nz,
    ny,
    grad_scale,
    pt_h,
    mo_h,
    gm_h,
    gp_h,
    wq_h,
    wk_h,
    wv_h,
    rf_h,
    ids_h,
    fi_o,
    gs_o,
    oq_o,
    ok_o,
    ov_o,
    xs,
    mo,
    gm,
    gp,
    w3,
    rf,
    ids,
    nrm,
    ntp,
    nts,
    qkv,
    fq,
    fk,
    pair,
    ga,
    dfk,
    dvl,
    dqkv,
    dqs,
    fmsg,
    fsib,
    fchip,
    fr,
    fs2,
    fst,
    foth,
    bmsg,
    bsib,
    bchip,
    br,
    bs2,
    bst,
    both,
    xso,
    xsm,
    xro,
    xrm,
    dots,
    dotr,
    qso,
    qsm,
    qro,
    qrm,
    kso,
    ksm,
    kro,
    krm,
    zqs,
    zqr,
    zks,
    zkr,
    lsem,
    ssem,
    rsem,
):
    seq = lax.axis_index("seq")
    x = lax.axis_index("head")
    y = lax.axis_index("dp")
    z = seq // 2
    c = seq % 2
    oc = 1 - c
    rw = D // (2 * nz * ny)
    rows_y = nz * rw
    right = lax.rem(x + 1, NX)
    left = lax.rem(x + NX - 1, NX)
    opp = lax.rem(x + 2, NX)

    def at_x(other):
        return (seq, other, y)

    def at_y(other):
        return (seq, x, other)

    def at_z(step):
        return (lax.rem(z + step + nz, nz) * 2 + c, x, y)

    sibling = (z * 2 + oc, x, y)

    barrier = pltpu.get_barrier_semaphore()
    peers = [sibling]
    peers += [at_x(lax.rem(x + d, NX)) for d in range(1, NX)]
    peers += [at_y(lax.rem(y + d, ny)) for d in range(1, ny)]
    peers += [at_z(d) for d in range(1, nz)]
    for peer in peers:
        pl.semaphore_signal(barrier, inc=1, device_id=peer, device_id_type=MESH)

    local = [
        pltpu.make_async_copy(src, dst, lsem.at[i])
        for i, (src, dst) in enumerate(
            [
                (pt_h.at[0], xs.at[0]),
                (ids_h, ids),
                (wk_h, w3.at[1]),
                (wv_h, w3.at[2]),
                (rf_h, rf),
                (wq_h, w3.at[0]),
                (gm_h.at[0], gm),
                (mo_h.at[0], mo),
                (gp_h.at[0], gp),
            ]
        )
    ]
    for copy in local:
        copy.start()

    counter = [0]
    pending = []

    def send(src, dst, device):
        i = counter[0]
        counter[0] += 1
        copy = pltpu.make_async_remote_copy(
            src_ref=src,
            dst_ref=dst,
            send_sem=ssem.at[i],
            recv_sem=rsem.at[i],
            device_id=device,
            device_id_type=MESH,
        )
        copy.start()
        pending.append(copy)
        return copy

    local[0].wait()
    pl.semaphore_wait(barrier, len(peers))

    top, bot = pl.ds(0, TOK // 2), pl.ds(TOK // 2, TOK // 2)
    l_top = send(xs.at[0, top], xs.at[1, top], at_x(right))
    r_bot = send(xs.at[0, bot], xs.at[3, bot], at_x(left))
    l_bot = send(xs.at[0, bot], xs.at[1, bot], at_x(right))
    r_top = send(xs.at[0, top], xs.at[3, top], at_x(left))

    local[1].wait()
    ids_row = jnp.broadcast_to(ids[...].astype(F32), (TOK, TOK))
    ids_col = ids_row.T
    tri = lax.broadcasted_iota(jnp.int32, (TOK, TOK), 0) >= lax.broadcasted_iota(
        jnp.int32, (TOK, TOK), 1
    )
    allowed = (ids_row == ids_col) & tri
    col_ids = ids_col[:, :HD]
    last_id = ids_row[:, TOK - 1 : TOK]
    first_id = ids_row[:, 0:1]
    is_last = col_ids == last_id
    is_first = col_ids == first_id
    last_rows = jnp.broadcast_to(last_id[:IDR], (IDR, HD)).astype(BF)
    first_rows = jnp.broadcast_to(first_id[:IDR], (IDR, HD)).astype(BF)

    l_top.wait_recv()
    o_top = send(xs.at[1, top], xs.at[2, top], at_x(right))
    r_bot.wait_recv()
    o_bot = send(xs.at[3, bot], xs.at[2, bot], at_x(left))

    def square_sum(slot):
        wide = xs[slot].astype(F32)
        return jnp.sum(wide * wide, axis=1, keepdims=True)

    squares = square_sum(0)
    l_bot.wait_recv()
    squares = squares + square_sum(1)
    r_top.wait_recv()
    squares = squares + square_sum(3)
    o_top.wait_recv()
    o_bot.wait_recv()
    squares = squares + square_sum(2)
    inv_rms = lax.rsqrt(squares * (1.0 / D) + EPSILON)
    for slot in range(NX):
        nrm[slot] = (xs[slot].astype(F32) * inv_rms).astype(BF)

    def source(slot):
        return lax.rem(x + NX - slot, NX)

    def project(which):
        total = None
        for slot in range(NX):
            rows = pl.ds(pl.multiple_of(source(slot) * WID, WID), WID)
            term = nn(nrm[slot], w3[which, rows, :])
            total = term if total is None else total + term
        return total.astype(BF)

    def features(head, projected):
        wide = projected.astype(F32)
        norm = jnp.sum(wide * wide, axis=1, keepdims=True)
        exponent = nn(projected, rf[head]) * (1.0 / HD**0.25) - norm * (1.0 / (2.0 * HD**0.5))
        return (jnp.exp(exponent) * (1.0 / FEAT**0.5)).astype(BF)

    local[2].wait()
    local[3].wait()
    local[4].wait()
    key = project(1)
    value = project(2)
    for head in range(2):
        cols = slice(head * HD, (head + 1) * HD)
        qkv[1, head] = key[:, cols]
        qkv[2, head] = value[:, cols]
        fk[head] = features(head, key[:, cols])
        masked = jnp.where(is_last, value[:, cols].astype(F32), 0.0).astype(BF)
        fmsg[head, 0:FEAT] = tn(fk[head], masked).astype(BF)
        fmsg[head, FEAT:MSG] = last_rows

    def merge(near, far):
        near_id, far_id = near[FEAT : FEAT + 1], far[FEAT : FEAT + 1]
        joined = near[:FEAT] + jnp.where(near_id == far_id, far[:FEAT], 0.0)
        return jnp.concatenate([joined, near[FEAT:]], axis=0)

    class Scan:
        def __init__(self, forward, msg, sib, chip, got, two, state, other):
            self.sign = 1 if forward else -1
            self.first = c == (0 if forward else 1)
            self.msg, self.sib, self.chip, self.got = msg, sib, chip, got
            self.two, self.state, self.other = two, state, other

        def begin(self):
            self.c0 = send(self.msg.at[oc], self.sib, sibling)

        def chips(self):
            self.c0.wait_recv()
            own, sib = self.msg[c].astype(F32), self.sib[...].astype(F32)
            upper = jnp.where(self.first, own, sib)
            lower = jnp.where(self.first, sib, own)
            self.chip[...] = merge(lower, upper).astype(BF)
            self.c1 = send(self.chip, self.got.at[0], at_z(self.sign))
            self.c2 = send(self.chip, self.got.at[1], at_z(2 * self.sign))

        def pairs(self):
            self.c1.wait_recv()
            self.c2.wait_recv()
            near, far = self.got[0].astype(F32), self.got[1].astype(F32)
            self.two[...] = merge(near, far).astype(BF)
            self.c3 = send(self.two, self.got.at[2], at_z(2 * self.sign))

        def spread(self):
            self.c3.wait_recv()
            own, sib = self.msg[c].astype(F32), self.sib[...].astype(F32)
            upper = jnp.where(self.first, own, sib)
            before = merge(self.two[...].astype(F32), self.got[2].astype(F32))
            after = merge(upper, before)
            self.state[c] = jnp.where(self.first, before, after).astype(BF)
            self.other[...] = jnp.where(self.first, after, before).astype(BF)
            self.c4 = send(self.other, self.state.at[c], sibling)

        def finish(self):
            self.c4.wait_recv()

    forward = Scan(True, fmsg, fsib, fchip, fr, fs2, fst, foth)
    forward.begin()

    local[5].wait()
    query = project(0)
    for head in range(2):
        cols = slice(head * HD, (head + 1) * HD)
        qkv[0, head] = query[:, cols]

    forward.chips()

    for head in range(2):
        fq[head] = features(head, qkv[0, head])
        scores = nt(fq[head], fk[head])
        pair[head] = jnp.where(allowed, scores, 0.0).astype(BF)

    forward.pairs()

    per_slot = nz // NX
    for slot in range(NX):
        turned = (xs[slot].astype(F32) * inv_rms).T.reshape(per_slot, 2, ny, rw, TOK)
        place = pl.ds(pl.multiple_of(source(slot) * (per_slot * rw), per_slot * rw), per_slot * rw)
        for core in range(2):
            for part in range(ny):
                block = turned[:, core, part].reshape(per_slot * rw, TOK)
                ntp[core, part, place, :] = block.astype(BF)
    c_nt = send(ntp.at[oc], nts, sibling)
    attn_local = [nn(pair[head], qkv[2, head]) for head in range(2)]

    forward.spread()
    local[6].wait()
    local[7].wait()
    forward.finish()

    for head in range(2):
        cols = slice(head * HD, (head + 1) * HD)
        on = col_ids == fst[head, FEAT : FEAT + 1, :].astype(F32)
        carried = nn(fq[head], fst[head, 0:FEAT, :])
        attention = attn_local[head] + jnp.where(on, carried, 0.0)
        inv_attn = lax.rsqrt(jnp.mean(attention * attention, axis=1, keepdims=True) + EPSILON)
        act = attention * inv_attn
        grad_act = gm[:, cols].astype(F32)
        inner = jnp.mean(grad_act * act, axis=1, keepdims=True)
        grad_wide = (inv_attn * (grad_act - act * inner)).astype(BF)
        ga[head] = grad_wide
        masked = jnp.where(is_first, grad_wide.astype(F32), 0.0).astype(BF)
        bmsg[head, 0:FEAT] = tn(fq[head], masked).astype(BF)
        bmsg[head, FEAT:MSG] = first_rows
        fi_o[0, :, cols] = (mo[:, cols].astype(F32) - act).astype(BF)

    backward = Scan(False, bmsg, bsib, bchip, br, bs2, bst, both)
    backward.begin()

    def feature_grad(dfeature, feature, projected, head):
        dexponent = dfeature * feature.astype(F32)
        back = nt(dexponent.astype(BF), rf[head])
        totals = jnp.sum(dexponent, axis=1, keepdims=True)
        result = back * (1.0 / HD**0.25) - projected.astype(F32) * (totals * (1.0 / HD**0.5))
        return result.astype(BF)

    dpairs = []
    for head in range(2):
        dscores = nt(ga[head], qkv[2, head])
        dpairs.append(jnp.where(allowed, dscores, 0.0).astype(BF))

    backward.chips()

    for head in range(2):
        cols = slice(head * HD, (head + 1) * HD)
        on = col_ids == fst[head, FEAT : FEAT + 1, :].astype(F32)
        masked = jnp.where(on, ga[head].astype(F32), 0.0).astype(BF)
        dfq = nn(dpairs[head], fk[head]) + nt(masked, fst[head, 0:FEAT, :])
        dqkv[0, :, cols] = feature_grad(dfq, fq[head], qkv[0, head], head)
    c_dq = send(dqkv.at[0], dqs.at[0], sibling)

    backward.pairs()

    for head in range(2):
        dfk[head] = tn(dpairs[head], fq[head])
        dvl[head] = tn(pair[head], ga[head])

    class Ring:
        def __init__(self, so, sm, ro, rm, to_right, to_left):
            self.so, self.sm, self.ro, self.rm = so, sm, ro, rm
            self.to_right, self.to_left = to_right, to_left
            self.half = so.shape[1]

        def opposite(self, block):
            self.so[0] = block[: self.half].astype(BF)
            self.so[1] = block[self.half :].astype(BF)
            self.o0 = send(self.so.at[0], self.ro.at[0], self.to_right)
            self.o1 = send(self.so.at[1], self.ro.at[1], self.to_left)

        def sides(self, to_right, to_left):
            self.sm[0, 1] = to_right[self.half :].astype(BF)
            self.m01 = send(self.sm.at[0, 1], self.rm.at[0, 1], self.to_right)
            self.sm[1, 0] = to_left[: self.half].astype(BF)
            self.m10 = send(self.sm.at[1, 0], self.rm.at[1, 0], self.to_left)
            self.r_top = to_right[: self.half]
            self.l_bot = to_left[self.half :]

        def relay(self):
            self.o0.wait_recv()
            self.sm[0, 0] = (self.r_top + self.ro[0].astype(F32)).astype(BF)
            self.m00 = send(self.sm.at[0, 0], self.rm.at[0, 0], self.to_right)
            self.o1.wait_recv()
            self.sm[1, 1] = (self.l_bot + self.ro[1].astype(F32)).astype(BF)
            self.m11 = send(self.sm.at[1, 1], self.rm.at[1, 1], self.to_left)

        def total(self, own):
            for copy in (self.m01, self.m10, self.m00, self.m11):
                copy.wait_recv()
            halves = [
                own[i * self.half : (i + 1) * self.half]
                + self.rm[0, i].astype(F32)
                + self.rm[1, i].astype(F32)
                for i in range(2)
            ]
            return jnp.concatenate(halves, axis=0)

    up, down = lax.rem(y + 1, ny), lax.rem(y + ny - 1, ny)

    def weight_rows(which, part):
        left_rows, right_rows = ntp[c, part], nts[part]
        term = nn(left_rows, dqkv[which]) + nn(right_rows, dqs[which])
        return term * grad_scale

    def y_block(whiches, part):
        return jnp.concatenate([weight_rows(which, part) for which in whiches], axis=1)

    def start_weights(ring, whiches):
        ring.opposite(y_block(whiches, lax.rem(y + 2, ny)))
        ring.sides(y_block(whiches, up), y_block(whiches, down))

    c_nt.wait_recv()
    c_dq.wait_recv()
    ring_q = Ring(qso, qsm, qro, qrm, at_y(up), at_y(down))
    if ny > 1:
        start_weights(ring_q, [0])
    own_q = y_block([0], y)

    backward.spread()
    if ny > 1:
        ring_q.relay()
    backward.finish()

    for head in range(2):
        cols = slice(head * HD, (head + 1) * HD)
        on = col_ids == bst[head, FEAT : FEAT + 1, :].astype(F32)
        later = bst[head, 0:FEAT, :]
        masked = jnp.where(on, qkv[2, head].astype(F32), 0.0).astype(BF)
        dfeat = dfk[head] + nt(masked, later)
        dqkv[2, :, cols] = (dvl[head] + jnp.where(on, nn(fk[head], later), 0.0)).astype(BF)
        dqkv[1, :, cols] = feature_grad(dfeat, fk[head], qkv[1, head], head)
    c_dkv = send(dqkv.at[pl.ds(1, 2)], dqs.at[pl.ds(1, 2)], sibling)

    def normed_term(owner, slot):
        rows = pl.ds(pl.multiple_of(owner * WID, WID), WID)
        term = nt(dqkv[0], w3[0, rows, :])
        term = term + nt(dqkv[1], w3[1, rows, :])
        term = term + nt(dqkv[2], w3[2, rows, :])
        return term, jnp.sum(term * xs[slot].astype(F32), axis=1, keepdims=True)

    ring_x = Ring(xso, xsm, xro, xrm, at_x(right), at_x(left))
    term, dot = normed_term(opp, 2)
    ring_x.opposite(term)
    term_r, dot_r = normed_term(right, 3)
    term_l, dot_l = normed_term(left, 1)
    ring_x.sides(term_r, term_l)

    c_dkv.wait_recv()
    ring_k = Ring(kso, ksm, kro, krm, at_y(up), at_y(down))
    if ny > 1:
        start_weights(ring_k, [1, 2])
    ring_x.relay()
    own_k = y_block([1, 2], y)

    term_own, dot_own = normed_term(x, 0)
    dot = (dot + dot_r + dot_l + dot_own) * inv_rms
    dots[...] = jnp.broadcast_to(dot, (TOK, HD)).T[:8]
    c_dot = [
        send(dots, dotr.at[d - 1], at_x(lax.rem(x + d, NX))) for d in range(1, NX)
    ]

    def z_send(out, got):
        copies = []
        for d in range(1, nz):
            to = lax.rem(z + d, nz)
            copies.append(send(out.at[to], got.at[d], at_z(d)))
        return copies

    def z_total(copies, out, got):
        total = out[z].astype(F32)
        for d in range(1, nz):
            copies[d - 1].wait_recv()
            total = total + got[d].astype(F32)
        return total

    total_q = ring_q.total(own_q) if ny > 1 else own_q
    total_q = total_q.reshape(nz, rw, WID)
    zqs[...] = jnp.concatenate([total_q[:, :, :HD], total_q[:, :, HD:]], axis=1).astype(BF)
    z_q = z_send(zqs, zqr)

    if ny > 1:
        ring_k.relay()

    for copy in c_dot:
        copy.wait_recv()
    dot_rows = dots[...] + dotr[0] + dotr[1] + dotr[2]
    dot_all = jnp.broadcast_to(dot_rows[0:1], (HD, TOK)).T
    local[8].wait()
    grad_normed = ring_x.total(term_own)
    norm_own = xs[0].astype(F32) * inv_rms
    mean = dot_all[:, 0:1] * (1.0 / D)
    gs_o[0] = (gp[...].astype(F32) + inv_rms * (grad_normed - norm_own * mean)).astype(BF)

    total_k = ring_k.total(own_k) if ny > 1 else own_k
    part_k = total_k[:, :WID].reshape(nz, rw, WID)
    part_v = total_k[:, WID:].reshape(nz, rw, WID)
    zks[...] = jnp.concatenate([part_k, part_v], axis=1).astype(BF)
    z_k = z_send(zks, zkr)

    sum_q = z_total(z_q, zqs, zqr)
    oq_o[...] = jnp.concatenate([sum_q[:rw], sum_q[rw:]], axis=1)
    sum_k = z_total(z_k, zks, zkr)
    ok_o[...] = sum_k[:rw]
    ov_o[...] = sum_k[rw:]

    for copy in pending:
        copy.wait_send()


def solution(mesh):
    nz = mesh.shape["seq"] // 2
    ny = mesh.shape["dp"]
    rw = D // (2 * nz * ny)
    rows_y = nz * rw

    def ring(rows, columns):
        half = rows // 2
        return [
            pltpu.VMEM((2, half, columns), BF),
            pltpu.VMEM((2, 2, half, columns), BF),
            pltpu.VMEM((2, half, columns), BF),
            pltpu.VMEM((2, 2, half, columns), BF),
        ]

    scan = [
        pltpu.VMEM((2, MSG, HD), BF),
        pltpu.VMEM((MSG, HD), BF),
        pltpu.VMEM((MSG, HD), BF),
        pltpu.VMEM((3, MSG, HD), BF),
        pltpu.VMEM((MSG, HD), BF),
        pltpu.VMEM((2, MSG, HD), BF),
        pltpu.VMEM((MSG, HD), BF),
    ]

    def shards(pt, mo, gm, gp, wq, wk, wv, rf, ids):
        total_rows = TOK * 2 * nz * ny
        copies = 100
        return pl.pallas_call(
            functools.partial(kernel, nz, ny, 1.0 / total_rows**0.5),
            out_shape=(
                jax.ShapeDtypeStruct((1, TOK, WID), BF),
                jax.ShapeDtypeStruct((1, TOK, WID), BF),
                jax.ShapeDtypeStruct((rw, WID), F32),
                jax.ShapeDtypeStruct((rw, WID), F32),
                jax.ShapeDtypeStruct((rw, WID), F32),
            ),
            in_specs=[pl.BlockSpec(memory_space=pl.ANY)] * 9,
            out_specs=[pl.BlockSpec(memory_space=pltpu.VMEM)] * 5,
            scratch_shapes=[
                pltpu.VMEM((NX, TOK, WID), BF),
                pltpu.VMEM((TOK, WID), BF),
                pltpu.VMEM((TOK, WID), BF),
                pltpu.VMEM((TOK, WID), BF),
                pltpu.VMEM((3, D, WID), BF),
                pltpu.VMEM((2, HD, FEAT), BF),
                pltpu.VMEM((1, TOK), jnp.int32),
                pltpu.VMEM((NX, TOK, WID), BF),
                pltpu.VMEM((2, ny, rows_y, TOK), BF),
                pltpu.VMEM((ny, rows_y, TOK), BF),
                pltpu.VMEM((3, 2, TOK, HD), BF),
                pltpu.VMEM((2, TOK, FEAT), BF),
                pltpu.VMEM((2, TOK, FEAT), BF),
                pltpu.VMEM((2, TOK, TOK), BF),
                pltpu.VMEM((2, TOK, HD), BF),
                pltpu.VMEM((2, TOK, FEAT), F32),
                pltpu.VMEM((2, TOK, HD), F32),
                pltpu.VMEM((3, TOK, WID), BF),
                pltpu.VMEM((3, TOK, WID), BF),
                *scan,
                *scan,
                *ring(TOK, WID),
                pltpu.VMEM((8, TOK), F32),
                pltpu.VMEM((NX - 1, 8, TOK), F32),
                *ring(rows_y, WID),
                *ring(rows_y, 2 * WID),
                pltpu.VMEM((nz, 2 * rw, HD), BF),
                pltpu.VMEM((nz, 2 * rw, HD), BF),
                pltpu.VMEM((nz, 2 * rw, WID), BF),
                pltpu.VMEM((nz, 2 * rw, WID), BF),
                pltpu.SemaphoreType.DMA((9,)),
                pltpu.SemaphoreType.DMA((copies,)),
                pltpu.SemaphoreType.DMA((copies,)),
            ],
            compiler_params=pltpu.CompilerParams(
                collective_id=0, has_side_effects=True, vmem_limit_bytes=48 * 1024 * 1024
            ),
            cost_estimate=pl.CostEstimate(
                flops=1_600_000_000, bytes_accessed=3_000_000, transcendentals=300_000
            ),
        )(pt, mo, gm, gp, wq, wk, wv, rf, ids)

    stream = P("dp", "seq", "head")
    return jax.shard_map(
        shards,
        mesh=mesh,
        in_specs=(
            stream,
            stream,
            stream,
            stream,
            P(None, "head"),
            P(None, "head"),
            P(None, "head"),
            P("head", None, None),
            P("dp", "seq"),
        ),
        out_specs=(
            stream,
            stream,
            P(("seq", "dp"), "head"),
            P(("seq", "dp"), "head"),
            P(("seq", "dp"), "head"),
        ),
        check_vma=False,
    )
```

time: 701 us -> 87.9 us (0.13); the launches traced: 689 us -> 87.5 us
  waiting for transfers between devices: 462 us -> 0 us
  Pallas kernels: 0 us -> 75.4 us
  blocking collectives: 73.8 us -> 0 us
  loops' own time: 61.4 us -> 0 us
  other arithmetic: 38.4 us -> 0 us
  between operations: 15.4 us -> 0.66 us
  matrix products: 14.5 us -> 0 us
  local copies, waits for them, and re-layouts: 23.3 us -> 11.4 us
    reduce_scatter x2 -> x0, waiting for transfers between devices: 268 us -> none  [the longest x1 249 us: shards(): lax.psum_scatter(jnp.einsum('ctr,ctj->rj', normed, grads_flat, preferred_...]
    all_gather x2 -> x0, waiting for transfers between devices: 194 us -> none  [carried_in(): lax.all_gather(a.astype(kind), axis)]
    pallas_call x0 -> x1, Pallas kernels: none -> 75.4 us  [shards(): pl.pallas_call(functools.partial(kernel, nz, ny, 1.0 / total_rows ** 0.5)...]
    another operation x2 -> x0, loops' own time: 61.4 us -> none  [carried_in(): return lax.fori_loop(0, ahead, one, state)]
    unnamed x1 -> x0, blocking collectives: 56.4 us -> none
    select_n x31 -> x0, other arithmetic: 32.2 us -> none  [join_state(): jnp.where(vacant, early_state, late_state + jnp.where(same_id, early_stat...]
    dynamic_slice x31 -> x0, local copies, waits for them, and re-layouts: 18.2 us -> none  [one(): lax.dynamic_index_in_dim(a, source, 0, False).astype(own.dtype)]
    dot_general x21 -> x0, matrix products: 14.5 us -> none  [the longest x1 2.78 us: shards(): jnp.einsum('ctj,dj->ctd', grads_flat, weights_all, preferred_element_type...]
  transfers between devices with their start and end apart: 4 -> 0, of which waited for: 4 -> 0; matrix products, arithmetic and copies ran while one was open for 2% -> 0% of each run, Pallas kernels for 0% -> 0%
where the time goes in v1:
time: 87.9 us; the launch traced here: 87.5 us
  Pallas kernels  75.4 us (86%)
  local copies, waits for them, and re-layouts  11.4 us (13%)
    pallas_call x1, Pallas kernels, shards(): pl.pallas_call(functools.partial(kernel, nz, ny, 1.0 / total_rows ** 0.5)...  75.4 us
    unnamed x23, local copies, waits for them, and re-layouts  11.4 us

profile of v1, /device:TPU:1, one launch (start us, length us, event | category | flops | bytes accessed | tf_op | source)
XLA Modules:
  0.0 87.5 jit_solution(8103534777593513309)
XLA Ops:
  0.6 0.0 copy-start
  0.6 1.0 %copy-done = bf16[1024,256]{1,0:T(8,128)(2,1)S(1)} copy-done((bf16[1024,256]{1,0:T(8,128)(2,1)S(1)}, bf16[1024,256]{1,0:T(8,128)(2,1)}, u32[]{:S(2)}) %copy-start) | copy-done | bytes 524312
  1.7 0.0 copy-start.1
  1.7 1.0 %copy-done.1 = bf16[1024,256]{1,0:T(8,128)(2,1)S(1)} copy-done((bf16[1024,256]{1,0:T(8,128)(2,1)S(1)}, bf16[1024,256]{1,0:T(8,128)(2,1)}, u32[]{:S(2)}) %copy-start.1) | copy-done | bytes 524312
  2.7 0.0 copy-start.2
  2.7 1.0 %copy-done.2 = bf16[1024,256]{1,0:T(8,128)(2,1)S(1)} copy-done((bf16[1024,256]{1,0:T(8,128)(2,1)S(1)}, bf16[1024,256]{1,0:T(8,128)(2,1)}, u32[]{:S(2)}) %copy-start.2) | copy-done | bytes 524312
  3.8 0.0 copy-start.3
  3.8 0.9 %copy-done.3 = bf16[1,256,256]{2,1,0:T(8,128)(2,1)S(1)} copy-done((bf16[1,256,256]{2,1,0:T(8,128)(2,1)S(1)}, bf16[1,256,256]{2,1,0:T(8,128)(2,1)}, u32[]{:S(2)}) %copy-start.3) | copy-done | bytes 131096
  4.7 0.0 copy-start.4
  4.7 0.9 %copy-done.4 = bf16[1,256,256]{2,1,0:T(8,128)(2,1)S(1)} copy-done((bf16[1,256,256]{2,1,0:T(8,128)(2,1)S(1)}, bf16[1,256,256]{2,1,0:T(8,128)(2,1)}, u32[]{:S(2)}) %copy-start.4) | copy-done | bytes 131096
  5.6 0.0 copy-start.5
  5.6 0.9 %copy-done.5 = bf16[1,256,256]{2,1,0:T(8,128)(2,1)S(1)} copy-done((bf16[1,256,256]{2,1,0:T(8,128)(2,1)S(1)}, bf16[1,256,256]{2,1,0:T(8,128)(2,1)}, u32[]{:S(2)}) %copy-start.5) | copy-done | bytes 131096
  6.5 0.0 copy-start.6
  6.5 0.9 %copy-done.6 = bf16[1,256,256]{2,1,0:T(8,128)(2,1)S(1)} copy-done((bf16[1,256,256]{2,1,0:T(8,128)(2,1)S(1)}, bf16[1,256,256]{2,1,0:T(8,128)(2,1)}, u32[]{:S(2)}) %copy-start.6) | copy-done | bytes 131096
  7.4 0.0 copy-start.7
  7.4 0.9 %copy-done.7 = bf16[2,128,256]{2,1,0:T(8,128)(2,1)S(1)} copy-done((bf16[2,128,256]{2,1,0:T(8,128)(2,1)S(1)}, bf16[2,128,256]{2,1,0:T(8,128)(2,1)}, u32[]{:S(2)}) %copy-start.7) | copy-done | bytes 131096
  8.3 0.0 copy-start.8
  8.3 0.7 copy-done.8
  9.0 75.4 %shard_map.128 = (bf16[1,256,256]{2,1,0:T(8,128)(2,1)S(1)}, bf16[1,256,256]{2,1,0:T(8,128)(2,1)S(1)}, f32[8,256]{1,0:T(8,128)S(1)}, f32[8,256]{1,0:T(8,128)S(1)}, f32[8,256]{1,0:T(8,128)S(1)}) custom-call(bf16[1,256,256]{2,1,0:T(8,128)(2,1)S(1)} %copy-done.3, bf16[1,256,256]{2,1,0:T(8,128)(2,1)S(1)} %copy-done.4, bf16[1,256,256]{2,1,0:T(8,128)(2,1)S(1)} %copy-done.5, ...), custom_call_target="tpu_custom_call" | custom-call | flops 1600000000 | bytes 3000000 | tf_op jit(solution)/shard_map/pallas_call | solution.py:557
  84.4 0.7 copy.19
  85.1 0.7 copy.20
  85.7 0.6 copy.21
  86.3 0.6 copy.22
  86.9 0.6 copy.23
Async XLA Ops:
  0.6 1.0 %copy-start = (bf16[1024,256]{1,0:T(8,128)(2,1)S(1)}, bf16[1024,256]{1,0:T(8,128)(2,1)}, u32[]{:S(2)}) copy-start(bf16[1024,256]{1,0:T(8,128)(2,1)} %wq_h.1) | copy-start | bytes 1572868
  1.7 1.0 %copy-start.1 = (bf16[1024,256]{1,0:T(8,128)(2,1)S(1)}, bf16[1024,256]{1,0:T(8,128)(2,1)}, u32[]{:S(2)}) copy-start(bf16[1024,256]{1,0:T(8,128)(2,1)} %wk_h.1) | copy-start | bytes 1572868
  2.7 1.0 %copy-start.2 = (bf16[1024,256]{1,0:T(8,128)(2,1)S(1)}, bf16[1024,256]{1,0:T(8,128)(2,1)}, u32[]{:S(2)}) copy-start(bf16[1024,256]{1,0:T(8,128)(2,1)} %wv_h.1) | copy-start | bytes 1572868
  3.8 0.9 %copy-start.3 = (bf16[1,256,256]{2,1,0:T(8,128)(2,1)S(1)}, bf16[1,256,256]{2,1,0:T(8,128)(2,1)}, u32[]{:S(2)}) copy-start(bf16[1,256,256]{2,1,0:T(8,128)(2,1)} %pt_h.1) | copy-start | bytes 393220
  4.7 0.9 %copy-start.4 = (bf16[1,256,256]{2,1,0:T(8,128)(2,1)S(1)}, bf16[1,256,256]{2,1,0:T(8,128)(2,1)}, u32[]{:S(2)}) copy-start(bf16[1,256,256]{2,1,0:T(8,128)(2,1)} %mo_h.1) | copy-start | bytes 393220
  5.6 0.9 %copy-start.5 = (bf16[1,256,256]{2,1,0:T(8,128)(2,1)S(1)}, bf16[1,256,256]{2,1,0:T(8,128)(2,1)}, u32[]{:S(2)}) copy-start(bf16[1,256,256]{2,1,0:T(8,128)(2,1)} %gm_h.1) | copy-start | bytes 393220
  6.5 0.9 %copy-start.6 = (bf16[1,256,256]{2,1,0:T(8,128)(2,1)S(1)}, bf16[1,256,256]{2,1,0:T(8,128)(2,1)}, u32[]{:S(2)}) copy-start(bf16[1,256,256]{2,1,0:T(8,128)(2,1)} %gp_h.1) | copy-start | bytes 393220
  7.4 0.9 %copy-start.7 = (bf16[2,128,256]{2,1,0:T(8,128)(2,1)S(1)}, bf16[2,128,256]{2,1,0:T(8,128)(2,1)}, u32[]{:S(2)}) copy-start(bf16[2,128,256]{2,1,0:T(8,128)(2,1)} %rf_h.1) | copy-start | bytes 393220
  8.3 0.7 copy-start.8

commit v2 on v1

v2 whole, which is shorter than its diff:
```python
import functools

import jax
import jax.numpy as jnp
from jax import lax
from jax.experimental import pallas as pl
from jax.experimental.pallas import tpu as pltpu
from jax.sharding import PartitionSpec as P

MESH = pl.DeviceIdType.MESH
BF = jnp.bfloat16
F32 = jnp.float32
EPSILON = 1e-06
TOK = 256
D = 1024
WID = 256
HD = 128
FEAT = 256
IDR = 16
PIECES = 2
CUT = FEAT // PIECES
MSG = CUT + IDR
NX = 4


def nn(a, b):
    return jnp.dot(a, b, preferred_element_type=F32)


def nt(a, b):
    return lax.dot_general(a, b, (((1,), (1,)), ((), ())), preferred_element_type=F32)


def tn(a, b):
    return lax.dot_general(a, b, (((0,), (0,)), ((), ())), preferred_element_type=F32)


def kernel(
    nz,
    ny,
    grad_scale,
    pt_h,
    mo_h,
    gm_h,
    gp_h,
    wq_h,
    wk_h,
    wv_h,
    rf_h,
    ids_h,
    fi_o,
    gs_o,
    wg_o,
    xs,
    moh,
    gmh,
    gp,
    w3,
    wkv,
    wqc,
    rf,
    ids,
    nrm,
    ntp,
    qb,
    kb,
    vb,
    fq,
    fk,
    pair,
    dpr,
    ga,
    dfk,
    dvl,
    dh,
    fib,
    fic,
    gsb,
    wgb,
    fmsg,
    fgot,
    ftwo,
    fst,
    bmsg,
    bgot,
    btwo,
    bst,
    xso,
    xsm,
    xro,
    xrm,
    dots,
    dotr,
    yso,
    ysm,
    yro,
    yrm,
    zs,
    zr,
    lsem,
    osem,
    ssem,
    rsem,
):
    seq = lax.axis_index("seq")
    x = lax.axis_index("head")
    y = lax.axis_index("dp")
    z = seq // 2
    c = seq % 2
    oc = 1 - c
    rw = D // (2 * nz * ny)
    right = lax.rem(x + 1, NX)
    left = lax.rem(x + NX - 1, NX)
    opp = lax.rem(x + 2, NX)
    up, down = lax.rem(y + 1, ny), lax.rem(y + ny - 1, ny)

    def at_x(other):
        return (seq, other, y)

    def at_y(other):
        return (seq, x, other)

    def at_z(step):
        return (lax.rem(z + step + nz, nz) * 2 + c, x, y)

    sibling = (z * 2 + oc, x, y)

    barrier = pltpu.get_barrier_semaphore()
    peers = [at_x(lax.rem(x + d, NX)) for d in range(1, NX)]
    peers += [sibling]
    peers += [at_z(d) for d in range(1, nz)]
    peers += [at_y(lax.rem(y + d, ny)) for d in range(1, ny)]
    for peer in peers:
        pl.semaphore_signal(barrier, inc=1, device_id=peer, device_id_type=MESH)

    mine = pl.ds(pl.multiple_of(c * HD, HD), HD)
    others = pl.ds(pl.multiple_of(oc * HD, HD), HD)
    local = {}
    for i, (name, src, dst) in enumerate(
        [
            ("pt", pt_h.at[0], xs.at[c, 0]),
            ("ids", ids_h, ids.at[c]),
            ("wk", wk_h.at[:, mine], wkv.at[:, pl.ds(0, HD)]),
            ("wv", wv_h.at[:, mine], wkv.at[:, pl.ds(HD, HD)]),
            ("rf", rf_h.at[c], rf),
            ("wq", wq_h.at[:, mine], wqc),
            ("gm", gm_h.at[0, :, mine], gmh.at[c]),
            ("mo", mo_h.at[0, :, mine], moh.at[c]),
            ("w0", wq_h, w3.at[0]),
            ("w1", wk_h, w3.at[1]),
            ("w2", wv_h, w3.at[2]),
            ("gp", gp_h.at[0], gp),
        ]
    ):
        local[name] = pltpu.make_async_copy(src, dst, lsem.at[i])
        local[name].start()

    counter = [0]
    pending = []

    def send(src, dst, device):
        i = counter[0]
        counter[0] += 1
        copy = pltpu.make_async_remote_copy(
            src_ref=src,
            dst_ref=dst,
            send_sem=ssem.at[i],
            recv_sem=rsem.at[i],
            device_id=device,
            device_id_type=MESH,
        )
        copy.start()
        pending.append(copy)
        return copy

    pl.semaphore_wait(barrier, len(peers))

    top, bot = pl.ds(0, TOK // 2), pl.ds(TOK // 2, TOK // 2)
    l_top = send(pt_h.at[0, top], xs.at[c, 1, top], at_x(right))
    r_bot = send(pt_h.at[0, bot], xs.at[c, 3, bot], at_x(left))
    l_bot = send(pt_h.at[0, bot], xs.at[c, 1, bot], at_x(right))
    r_top = send(pt_h.at[0, top], xs.at[c, 3, top], at_x(left))
    passed = [send(pt_h.at[0], xs.at[c, 0], sibling)]
    c_ids = send(ids_h, ids.at[c], sibling)
    c_gm = send(gm_h.at[0, :, others], gmh.at[c], sibling)
    c_mo = send(mo_h.at[0, :, others], moh.at[c], sibling)

    def pass_on(slot, rows):
        passed.append(send(xs.at[c, slot, rows], xs.at[c, slot, rows], sibling))

    l_top.wait_recv()
    o_top = send(xs.at[c, 1, top], xs.at[c, 2, top], at_x(right))
    pass_on(1, top)
    r_bot.wait_recv()
    o_bot = send(xs.at[c, 3, bot], xs.at[c, 2, bot], at_x(left))
    pass_on(3, bot)

    local["ids"].wait()
    c_ids.wait_recv()
    row_ids, col_ids = [], []
    for b in range(2):
        row_ids.append(jnp.broadcast_to(ids[b].astype(F32), (TOK, TOK)))
        col_ids.append(row_ids[b].T)
    tri = lax.broadcasted_iota(jnp.int32, (TOK, TOK), 0) >= lax.broadcasted_iota(
        jnp.int32, (TOK, TOK), 1
    )
    chip_last = row_ids[1][:, TOK - 1 : TOK]
    chip_first = row_ids[0][:, 0:1]
    last_rows = jnp.broadcast_to(chip_last[:IDR], (IDR, HD)).astype(BF)
    first_rows = jnp.broadcast_to(chip_first[:IDR], (IDR, HD)).astype(BF)
    for i in range(PIECES):
        fmsg[i, CUT:MSG] = last_rows
        bmsg[i, CUT:MSG] = first_rows

    def on_rows(b, ident):
        return col_ids[b][:, :HD] == ident

    def square_sum(b, slot):
        wide = xs[b, slot].astype(F32)
        return jnp.sum(wide * wide, axis=1, keepdims=True)

    def normalize(b, squares):
        inv = lax.rsqrt(squares * (1.0 / D) + EPSILON)
        for slot in range(NX):
            nrm[b, slot] = (xs[b, slot].astype(F32) * inv).astype(BF)
        return inv

    def source(slot):
        return lax.rem(x + NX - slot, NX)

    def project(b, weights):
        total = None
        for slot in range(NX):
            rows = pl.ds(pl.multiple_of(source(slot) * WID, WID), WID)
            term = nn(nrm[b, slot], weights[rows, :])
            total = term if total is None else total + term
        return total.astype(BF)

    def features(projected):
        wide = projected.astype(F32)
        norm = jnp.sum(wide * wide, axis=1, keepdims=True)
        exponent = nn(projected, rf[...]) * (1.0 / HD**0.25) - norm * (1.0 / (2.0 * HD**0.5))
        return (jnp.exp(exponent) * (1.0 / FEAT**0.5)).astype(BF)

    def keys_values(b):
        both = project(b, wkv)
        kb[b] = both[:, :HD]
        vb[b] = both[:, HD:]
        fk[b] = features(both[:, :HD])

    local["pt"].wait()
    squares = square_sum(c, 0)
    l_bot.wait_recv()
    pass_on(1, bot)
    r_top.wait_recv()
    pass_on(3, top)
    squares = squares + square_sum(c, 1) + square_sum(c, 3)
    o_top.wait_recv()
    pass_on(2, top)
    o_bot.wait_recv()
    pass_on(2, bot)
    squares = squares + square_sum(c, 2)
    inv_rms = normalize(c, squares)
    local["wk"].wait()
    local["wv"].wait()
    local["rf"].wait()
    keys_values(c)
    for copy in passed:
        copy.wait_recv()
    squares = square_sum(oc, 0) + square_sum(oc, 1) + square_sum(oc, 3) + square_sum(oc, 2)
    normalize(oc, squares)
    keys_values(oc)

    def outer_sum(left_ref, right_ref, ident):
        total = None
        for b in range(2):
            masked = jnp.where(on_rows(b, ident), right_ref[b].astype(F32), 0.0).astype(BF)
            term = tn(left_ref[b], masked)
            total = term if total is None else total + term
        return total.astype(BF)

    def merge(near, far):
        return near[:CUT] + jnp.where(near[CUT : CUT + 1] == far[CUT : CUT + 1], far[:CUT], 0.0)

    class Scan:
        def __init__(self, sign, msg, got, two, state):
            self.sign, self.msg, self.got, self.two, self.state = sign, msg, got, two, state

        def begin(self, outer):
            self.near, self.far = [], []
            for i in range(PIECES):
                self.msg[i, 0:CUT] = outer[i * CUT : (i + 1) * CUT]
                self.near.append(send(self.msg.at[i], self.got.at[0, i], at_z(self.sign)))
                self.far.append(send(self.msg.at[i], self.got.at[1, i], at_z(2 * self.sign)))

        def pairs(self):
            self.last = []
            for i in range(PIECES):
                self.near[i].wait_recv()
                self.far[i].wait_recv()
                near, far = self.got[0, i].astype(F32), self.got[1, i].astype(F32)
                self.two[i, 0:CUT] = merge(near, far).astype(BF)
                self.two[i, CUT:MSG] = self.got[0, i, CUT:MSG]
                self.last.append(send(self.two.at[i], self.got.at[2, i], at_z(2 * self.sign)))

        def finish(self):
            for i in range(PIECES):
                self.last[i].wait_recv()
                near, far = self.two[i].astype(F32), self.got[2, i].astype(F32)
                self.state[i * CUT : (i + 1) * CUT] = merge(near, far).astype(BF)
            return self.two[0, CUT : CUT + 1].astype(F32)

    forward = Scan(1, fmsg, fgot, ftwo, fst)
    forward.begin(outer_sum(fk, vb, chip_last))

    local["wq"].wait()
    for b in range(2):
        qb[b] = project(b, wqc)
        fq[b] = features(qb[b])

    forward.pairs()

    blocks = [(0, 0), (1, 0), (1, 1)]
    allowed = []
    for i, (b, s) in enumerate(blocks):
        same = row_ids[s] == col_ids[b]
        allowed.append(same & tri if b == s else same)
        pair[i] = jnp.where(allowed[i], nt(fq[b], fk[s]), 0.0).astype(BF)
    attn = [nn(pair[0], vb[0]), nn(pair[1], vb[0]) + nn(pair[2], vb[1])]

    per_slot = nz // NX
    for slot in range(NX):
        place = pl.ds(pl.multiple_of(source(slot) * (per_slot * rw), per_slot * rw), per_slot * rw)
        for b in range(2):
            turned = nrm[b, slot].astype(F32).T.reshape(per_slot, 2, ny, rw, TOK)
            turned = jnp.where(c == 0, turned[:, 0], turned[:, 1])
            for part in range(ny):
                block = turned[:, part].reshape(per_slot * rw, TOK)
                ntp[part, place, b * TOK : (b + 1) * TOK] = block.astype(BF)

    local["gm"].wait()
    local["mo"].wait()
    c_gm.wait_recv()
    c_mo.wait_recv()
    f_id = forward.finish()

    acts = []
    for b in range(2):
        attention = attn[b] + jnp.where(on_rows(b, f_id), nn(fq[b], fst[...]), 0.0)
        inv_attn = lax.rsqrt(jnp.mean(attention * attention, axis=1, keepdims=True) + EPSILON)
        act = attention * inv_attn
        acts.append(act)
        grad_act = gmh[b].astype(F32)
        inner = jnp.mean(grad_act * act, axis=1, keepdims=True)
        ga[b] = (inv_attn * (grad_act - act * inner)).astype(BF)

    backward = Scan(-1, bmsg, bgot, btwo, bst)
    backward.begin(outer_sum(fq, ga, chip_first))

    for b in range(2):
        fib[b] = (moh[b].astype(F32) - acts[b]).astype(BF)
    c_fi = send(fib.at[oc], fic, sibling)
    out_fi = pltpu.make_async_copy(fib.at[c], fi_o.at[0, :, mine], osem.at[0])
    out_fi.start()

    def feature_grad(dfeature, feature, projected):
        dexponent = dfeature * feature.astype(F32)
        back = nt(dexponent.astype(BF), rf[...])
        totals = jnp.sum(dexponent, axis=1, keepdims=True)
        result = back * (1.0 / HD**0.25) - projected.astype(F32) * (totals * (1.0 / HD**0.5))
        return result.astype(BF)

    for i, (b, s) in enumerate(blocks):
        dpr[i] = jnp.where(allowed[i], nt(ga[b], vb[s]), 0.0).astype(BF)
    dfq = [nn(dpr[0], fk[0]), nn(dpr[1], fk[0]) + nn(dpr[2], fk[1])]

    backward.pairs()

    for b in range(2):
        masked = jnp.where(on_rows(b, f_id), ga[b].astype(F32), 0.0).astype(BF)
        dfeat = dfq[b] + nt(masked, fst[...])
        dh[0, b * TOK : (b + 1) * TOK, mine] = feature_grad(dfeat, fq[b], qb[b])
    c_dq = send(dh.at[0, :, mine], dh.at[0, :, mine], sibling)

    dfk[0] = tn(dpr[0], fq[0]) + tn(dpr[1], fq[1])
    dfk[1] = tn(dpr[2], fq[1])
    dvl[0] = tn(pair[0], ga[0]) + tn(pair[1], ga[1])
    dvl[1] = tn(pair[2], ga[1])

    class Ring:
        def __init__(self, so, sm, ro, rm, to_right, to_left):
            self.so, self.sm, self.ro, self.rm = so, sm, ro, rm
            self.to_right, self.to_left = to_right, to_left
            self.half = so.shape[1]

        def opposite(self, block):
            self.so[0] = block[: self.half].astype(BF)
            self.o0 = send(self.so.at[0], self.ro.at[0], self.to_right)
            self.so[1] = block[self.half :].astype(BF)
            self.o1 = send(self.so.at[1], self.ro.at[1], self.to_left)

        def sides(self, to_right, to_left):
            self.sm[0, 1] = to_right[self.half :].astype(BF)
            self.m01 = send(self.sm.at[0, 1], self.rm.at[0, 1], self.to_right)
            self.sm[1, 0] = to_left[: self.half].astype(BF)
            self.m10 = send(self.sm.at[1, 0], self.rm.at[1, 0], self.to_left)
            self.r_top = to_right[: self.half]
            self.l_bot = to_left[self.half :]

        def relay(self):
            self.o0.wait_recv()
            self.sm[0, 0] = (self.r_top + self.ro[0].astype(F32)).astype(BF)
            self.m00 = send(self.sm.at[0, 0], self.rm.at[0, 0], self.to_right)
            self.o1.wait_recv()
            self.sm[1, 1] = (self.l_bot + self.ro[1].astype(F32)).astype(BF)
            self.m11 = send(self.sm.at[1, 1], self.rm.at[1, 1], self.to_left)

        def total(self, own):
            for copy in (self.m01, self.m10, self.m00, self.m11):
                copy.wait_recv()
            halves = [
                own[i * self.half : (i + 1) * self.half]
                + self.rm[0, i].astype(F32)
                + self.rm[1, i].astype(F32)
                for i in range(2)
            ]
            return jnp.concatenate(halves, axis=0)

    def y_ring(which):
        return Ring(yso.at[which], ysm.at[which], yro.at[which], yrm.at[which], at_y(up), at_y(down))

    def weight_rows(which, part):
        return nn(ntp[part], dh[which]) * grad_scale

    def start_weights(which):
        ring = y_ring(which)
        ring.opposite(weight_rows(which, lax.rem(y + 2, ny)))
        ring.sides(weight_rows(which, up), weight_rows(which, down))
        return ring

    def z_send(which, total):
        split = total.reshape(nz, rw, WID)
        zs[which] = jnp.concatenate([split[:, :, :HD], split[:, :, HD:]], axis=1).astype(BF)
        copies = []
        for d in range(1, nz):
            to = lax.rem(z + d, nz)
            copies.append(send(zs.at[which, to], zr.at[which, d], at_z(d)))
        return copies

    def z_total(which, copies):
        total = zs[which, z].astype(F32)
        for d in range(1, nz):
            copies[d - 1].wait_recv()
            total = total + zr[which, d].astype(F32)
        wgb[which] = jnp.concatenate([total[:rw], total[rw:]], axis=1)

    c_dq.wait_recv()
    ring_q = start_weights(0)
    own_q = weight_rows(0, y)

    b_id = backward.finish()

    for b in range(2):
        carried = jnp.where(on_rows(b, b_id), nn(fk[b], bst[...]), 0.0)
        dh[2, b * TOK : (b + 1) * TOK, mine] = (dvl[b] + carried).astype(BF)
    c_dv = send(dh.at[2, :, mine], dh.at[2, :, mine], sibling)
    for b in range(2):
        masked = jnp.where(on_rows(b, b_id), vb[b].astype(F32), 0.0).astype(BF)
        dfeat = dfk[b] + nt(masked, bst[...])
        dh[1, b * TOK : (b + 1) * TOK, mine] = feature_grad(dfeat, fk[b], kb[b])
    c_dk = send(dh.at[1, :, mine], dh.at[1, :, mine], sibling)
    ring_q.relay()
    local["w0"].wait()
    local["w1"].wait()
    local["w2"].wait()

    c_dv.wait_recv()
    ring_v = start_weights(2)
    c_dk.wait_recv()
    ring_k = start_weights(1)

    own_rows = pl.ds(pl.multiple_of(c * TOK, TOK), TOK)

    def normed_term(owner, slot):
        rows = pl.ds(pl.multiple_of(owner * WID, WID), WID)
        term = nt(dh[0, own_rows, :], w3[0, rows, :])
        term = term + nt(dh[1, own_rows, :], w3[1, rows, :])
        term = term + nt(dh[2, own_rows, :], w3[2, rows, :])
        return term, jnp.sum(term * xs[c, slot].astype(F32), axis=1, keepdims=True)

    ring_x = Ring(xso, xsm, xro, xrm, at_x(right), at_x(left))
    term, dot = normed_term(opp, 2)
    ring_x.opposite(term)
    term_r, dot_r = normed_term(right, 3)
    term_l, dot_l = normed_term(left, 1)
    ring_x.sides(term_r, term_l)

    ring_v.relay()
    z_q = z_send(0, ring_q.total(own_q))
    ring_k.relay()
    ring_x.relay()

    term_own, dot_own = normed_term(x, 0)
    dot = (dot + dot_r + dot_l + dot_own) * inv_rms
    dots[...] = jnp.broadcast_to(dot, (TOK, HD)).T[:8]
    c_dot = [send(dots, dotr.at[d - 1], at_x(lax.rem(x + d, NX))) for d in range(1, NX)]
    own_v = weight_rows(2, y)
    own_k = weight_rows(1, y)

    z_v = z_send(2, ring_v.total(own_v))
    z_k = z_send(1, ring_k.total(own_k))

    for copy in c_dot:
        copy.wait_recv()
    dot_rows = dots[...] + dotr[0] + dotr[1] + dotr[2]
    dot_all = jnp.broadcast_to(dot_rows[0:1], (HD, TOK)).T
    local["gp"].wait()
    grad_normed = ring_x.total(term_own)
    norm_own = xs[c, 0].astype(F32) * inv_rms
    mean = dot_all[:, 0:1] * (1.0 / D)
    gsb[...] = (gp[...].astype(F32) + inv_rms * (grad_normed - norm_own * mean)).astype(BF)
    out_gs = pltpu.make_async_copy(gsb, gs_o.at[0], osem.at[1])
    out_gs.start()
    c_fi.wait_recv()
    out_fi2 = pltpu.make_async_copy(fic, fi_o.at[0, :, others], osem.at[2])
    out_fi2.start()

    z_total(0, z_q)
    z_total(2, z_v)
    z_total(1, z_k)
    out_wg = pltpu.make_async_copy(wgb, wg_o, osem.at[3])
    out_wg.start()
    for copy in (out_fi, out_gs, out_fi2, out_wg):
        copy.wait()
    for copy in pending:
        copy.wait_send()


def hand_out(fi, gs, wg, fi_o, gs_o, q_o, k_o, v_o, sem):
    copies = [
        pltpu.make_async_copy(src, dst, sem.at[i])
        for i, (src, dst) in enumerate(
            [(fi, fi_o), (gs, gs_o), (wg.at[0], q_o), (wg.at[1], k_o), (wg.at[2], v_o)]
        )
    ]
    for copy in copies:
        copy.start()
    for copy in copies:
        copy.wait()


def solution(mesh):
    nz = mesh.shape["seq"] // 2
    ny = mesh.shape["dp"]
    rw = D // (2 * nz * ny)
    rows_y = nz * rw
    half = rows_y // 2

    scan = [
        pltpu.VMEM((PIECES, MSG, HD), BF),
        pltpu.VMEM((3, PIECES, MSG, HD), BF),
        pltpu.VMEM((PIECES, MSG, HD), BF),
        pltpu.VMEM((FEAT, HD), BF),
    ]

    def shards(pt, mo, gm, gp, wq, wk, wv, rf, ids):
        total_rows = TOK * 2 * nz * ny
        copies = 110
        stream = jax.ShapeDtypeStruct((1, TOK, WID), BF)
        grads = jax.ShapeDtypeStruct((rw, WID), F32)
        limit = pltpu.CompilerParams(
            collective_id=0, has_side_effects=True, vmem_limit_bytes=58 * 1024 * 1024
        )
        first_in, grad_second, weights = pl.pallas_call(
            functools.partial(kernel, nz, ny, 1.0 / total_rows**0.5),
            out_shape=(stream, stream, jax.ShapeDtypeStruct((3, rw, WID), F32)),
            in_specs=[pl.BlockSpec(memory_space=pl.ANY)] * 9,
            out_specs=[pl.BlockSpec(memory_space=pl.ANY)] * 3,
            scratch_shapes=[
                pltpu.VMEM((2, NX, TOK, WID), BF),
                pltpu.VMEM((2, TOK, HD), BF),
                pltpu.VMEM((2, TOK, HD), BF),
                pltpu.VMEM((TOK, WID), BF),
                pltpu.VMEM((3, D, WID), BF),
                pltpu.VMEM((D, WID), BF),
                pltpu.VMEM((D, HD), BF),
                pltpu.VMEM((HD, FEAT), BF),
                pltpu.VMEM((2, 1, TOK), jnp.int32),
                pltpu.VMEM((2, NX, TOK, WID), BF),
                pltpu.VMEM((ny, rows_y, 2 * TOK), BF),
                pltpu.VMEM((2, TOK, HD), BF),
                pltpu.VMEM((2, TOK, HD), BF),
                pltpu.VMEM((2, TOK, HD), BF),
                pltpu.VMEM((2, TOK, FEAT), BF),
                pltpu.VMEM((2, TOK, FEAT), BF),
                pltpu.VMEM((3, TOK, TOK), BF),
                pltpu.VMEM((3, TOK, TOK), BF),
                pltpu.VMEM((2, TOK, HD), BF),
                pltpu.VMEM((2, TOK, FEAT), F32),
                pltpu.VMEM((2, TOK, HD), F32),
                pltpu.VMEM((3, 2 * TOK, WID), BF),
                pltpu.VMEM((2, TOK, HD), BF),
                pltpu.VMEM((TOK, HD), BF),
                pltpu.VMEM((TOK, WID), BF),
                pltpu.VMEM((3, rw, WID), F32),
                *scan,
                *scan,
                pltpu.VMEM((2, TOK // 2, WID), BF),
                pltpu.VMEM((2, 2, TOK // 2, WID), BF),
                pltpu.VMEM((2, TOK // 2, WID), BF),
                pltpu.VMEM((2, 2, TOK // 2, WID), BF),
                pltpu.VMEM((8, TOK), F32),
                pltpu.VMEM((NX - 1, 8, TOK), F32),
                pltpu.VMEM((3, 2, half, WID), BF),
                pltpu.VMEM((3, 2, 2, half, WID), BF),
                pltpu.VMEM((3, 2, half, WID), BF),
                pltpu.VMEM((3, 2, 2, half, WID), BF),
                pltpu.VMEM((3, nz, 2 * rw, HD), BF),
                pltpu.VMEM((3, nz, 2 * rw, HD), BF),
                pltpu.SemaphoreType.DMA((12,)),
                pltpu.SemaphoreType.DMA((4,)),
                pltpu.SemaphoreType.DMA((copies,)),
                pltpu.SemaphoreType.DMA((copies,)),
            ],
            compiler_params=limit,
            cost_estimate=pl.CostEstimate(
                flops=1_800_000_000, bytes_accessed=4_000_000, transcendentals=300_000
            ),
        )(pt, mo, gm, gp, wq, wk, wv, rf, ids)
        return pl.pallas_call(
            hand_out,
            out_shape=(stream, stream, grads, grads, grads),
            in_specs=[pl.BlockSpec(memory_space=pl.ANY)] * 3,
            out_specs=[pl.BlockSpec(memory_space=pl.ANY)] * 5,
            scratch_shapes=[pltpu.SemaphoreType.DMA((5,))],
            compiler_params=pltpu.CompilerParams(vmem_limit_bytes=58 * 1024 * 1024),
        )(first_in, grad_second, weights)

    stream = P("dp", "seq", "head")
    return jax.shard_map(
        shards,
        mesh=mesh,
        in_specs=(
            stream,
            stream,
            stream,
            stream,
            P(None, "head"),
            P(None, "head"),
            P(None, "head"),
            P("head", None, None),
            P("dp", "seq"),
        ),
        out_specs=(
            stream,
            stream,
            P(("seq", "dp"), "head"),
            P(("seq", "dp"), "head"),
            P(("seq", "dp"), "head"),
        ),
        check_vma=False,
    )
```

time: 87.9 us -> 82.3 us (0.936)
  local copies, waits for them, and re-layouts: 11.4 us -> 0 us
  Pallas kernels: 75.4 us -> 81.6 us
    unnamed x23 -> x0, local copies, waits for them, and re-layouts: 11.4 us -> none
    pallas_call x0 -> x1, Pallas kernels: none -> 9.83 us  [shards(): pl.pallas_call(hand_out, out_shape=(stream, stream, grads, grads, grads),...]
    pallas_call x1, Pallas kernels: 75.4 us -> 71.8 us  [shards(): pl.pallas_call(functools.partial(kernel, nz, ny, 1.0 / total_rows ** 0.5)...]
where the time goes in v2:
time: 82.3 us; the launch traced here: 82.2 us
  Pallas kernels  81.6 us (99%)
    pallas_call x1, Pallas kernels, shards(): pl.pallas_call(functools.partial(kernel, nz, ny, 1.0 / total_rows ** 0.5)...  71.8 us
    pallas_call x1, Pallas kernels, shards(): pl.pallas_call(hand_out, out_shape=(stream, stream, grads, grads, grads),...  9.83 us

profile of v2, /device:TPU:1, one launch (start us, length us, event | category | flops | bytes accessed | tf_op | source)
XLA Modules:
  0.0 82.2 jit_solution(17885495745503421682)
XLA Ops:
  0.6 71.8 %shard_map.128 = (bf16[1,256,256]{2,1,0:T(8,128)(2,1)}, bf16[1,256,256]{2,1,0:T(8,128)(2,1)}, f32[3,8,256]{2,1,0:T(8,128)}) custom-call(bf16[1,256,256]{2,1,0:T(8,128)(2,1)} %pt_h.1, bf16[1,256,256]{2,1,0:T(8,128)(2,1)} %mo_h.1, bf16[1,256,256]{2,1,0:T(8,128)(2,1)} %gm_h.1, bf16[1,256,256]{2,1,0:T(8,128)(2,1)} %gp_h.1, bf16[1024,256]{1,0:T(8,128)(2,1)} %wq_h.1, ...), custom_call_target="tpu_custom_call" | custom-call | flops 1800000000 | bytes 4000000 | tf_op jit(solution)/shard_map/pallas_call | solution.py:574
  72.4 9.8 %shard_map.129 = (bf16[1,256,256]{2,1,0:T(8,128)(2,1)}, bf16[1,256,256]{2,1,0:T(8,128)(2,1)}, f32[8,256]{1,0:T(8,128)}, f32[8,256]{1,0:T(8,128)}, f32[8,256]{1,0:T(8,128)}) custom-call(bf16[1,256,256]{2,1,0:T(8,128)(2,1)} %get-tuple-element.8.fi, bf16[1,256,256]{2,1,0:T(8,128)(2,1)} %get-tuple-element.9.gs, f32[3,8,256]{2,1,0:T(8,128)} %get-tuple-element.10.wg), custom_call_target="tpu_custom_call" | custom-call | tf_op jit(solution)/shard_map/pallas_call | solution.py:630

commit v3 on v2

--- a/solution.py
+++ b/solution.py
@@ -153,7 +153,6 @@
         ]
     ):
         local[name] = pltpu.make_async_copy(src, dst, lsem.at[i])
-        local[name].start()
 
     counter = [0]
     pending = []
@@ -173,6 +172,9 @@
         pending.append(copy)
         return copy
 
+    early = ("pt", "ids")
+    for name in early:
+        local[name].start()
     pl.semaphore_wait(barrier, len(peers))
 
     top, bot = pl.ds(0, TOK // 2), pl.ds(TOK // 2, TOK // 2)
@@ -182,6 +184,9 @@
     r_top = send(pt_h.at[0, top], xs.at[c, 3, top], at_x(left))
     passed = [send(pt_h.at[0], xs.at[c, 0], sibling)]
     c_ids = send(ids_h, ids.at[c], sibling)
+    for name, copy in local.items():
+        if name not in early:
+            copy.start()
     c_gm = send(gm_h.at[0, :, others], gmh.at[c], sibling)
     c_mo = send(mo_h.at[0, :, others], moh.at[c], sibling)
 
@@ -357,12 +362,6 @@
     backward = Scan(-1, bmsg, bgot, btwo, bst)
     backward.begin(outer_sum(fq, ga, chip_first))
 
-    for b in range(2):
-        fib[b] = (moh[b].astype(F32) - acts[b]).astype(BF)
-    c_fi = send(fib.at[oc], fic, sibling)
-    out_fi = pltpu.make_async_copy(fib.at[c], fi_o.at[0, :, mine], osem.at[0])
-    out_fi.start()
-
     def feature_grad(dfeature, feature, projected):
         dexponent = dfeature * feature.astype(F32)
         back = nt(dexponent.astype(BF), rf[...])
@@ -374,8 +373,6 @@
         dpr[i] = jnp.where(allowed[i], nt(ga[b], vb[s]), 0.0).astype(BF)
     dfq = [nn(dpr[0], fk[0]), nn(dpr[1], fk[0]) + nn(dpr[2], fk[1])]
 
-    backward.pairs()
-
     for b in range(2):
         masked = jnp.where(on_rows(b, f_id), ga[b].astype(F32), 0.0).astype(BF)
         dfeat = dfq[b] + nt(masked, fst[...])
@@ -386,6 +383,8 @@
     dfk[1] = tn(dpr[2], fq[1])
     dvl[0] = tn(pair[0], ga[0]) + tn(pair[1], ga[1])
     dvl[1] = tn(pair[2], ga[1])
+
+    backward.pairs()
 
     class Ring:
         def __init__(self, so, sm, ro, rm, to_right, to_left):
@@ -456,7 +455,15 @@
 
     c_dq.wait_recv()
     ring_q = start_weights(0)
+
+    for b in range(2):
+        fib[b] = (moh[b].astype(F32) - acts[b]).astype(BF)
+    c_fi = send(fib.at[oc], fic, sibling)
+    out_fi = pltpu.make_async_copy(fib.at[c], fi_o.at[0, :, mine], osem.at[0])
+    out_fi.start()
+
     own_q = weight_rows(0, y)
+    ring_q.relay()
 
     b_id = backward.finish()
 
@@ -469,7 +476,7 @@
         dfeat = dfk[b] + nt(masked, bst[...])
         dh[1, b * TOK : (b + 1) * TOK, mine] = feature_grad(dfeat, fk[b], kb[b])
     c_dk = send(dh.at[1, :, mine], dh.at[1, :, mine], sibling)
-    ring_q.relay()
+    z_q = z_send(0, ring_q.total(own_q))
     local["w0"].wait()
     local["w1"].wait()
     local["w2"].wait()
@@ -496,7 +503,6 @@
     ring_x.sides(term_r, term_l)
 
     ring_v.relay()
-    z_q = z_send(0, ring_q.total(own_q))
     ring_k.relay()
     ring_x.relay()
 
@@ -536,16 +542,20 @@
         copy.wait_send()
 
 
-def hand_out(fi, gs, wg, fi_o, gs_o, q_o, k_o, v_o, sem):
-    copies = [
-        pltpu.make_async_copy(src, dst, sem.at[i])
-        for i, (src, dst) in enumerate(
-            [(fi, fi_o), (gs, gs_o), (wg.at[0], q_o), (wg.at[1], k_o), (wg.at[2], v_o)]
-        )
-    ]
-    for copy in copies:
+def hand_out(fi, gs, wg, fi_o, gs_o, q_o, k_o, v_o, fi_v, gs_v, wg_v, isem, osem):
+    arrive = [(fi, fi_v), (gs, gs_v), (wg, wg_v)]
+    leave = [(fi_v, fi_o), (gs_v, gs_o), (wg_v.at[0], q_o), (wg_v.at[1], k_o), (wg_v.at[2], v_o)]
+    taken = [pltpu.make_async_copy(a, b, isem.at[i]) for i, (a, b) in enumerate(arrive)]
+    given = [pltpu.make_async_copy(a, b, osem.at[i]) for i, (a, b) in enumerate(leave)]
+    for copy in taken:
         copy.start()
-    for copy in copies:
+    for i in range(2):
+        taken[i].wait()
+        given[i].start()
+    taken[2].wait()
+    for copy in given[2:]:
+        copy.start()
+    for copy in given:
         copy.wait()
 
 
@@ -632,7 +642,13 @@
             out_shape=(stream, stream, grads, grads, grads),
             in_specs=[pl.BlockSpec(memory_space=pl.ANY)] * 3,
             out_specs=[pl.BlockSpec(memory_space=pl.ANY)] * 5,
-            scratch_shapes=[pltpu.SemaphoreType.DMA((5,))],
+            scratch_shapes=[
+                pltpu.VMEM((1, TOK, WID), BF),
+                pltpu.VMEM((1, TOK, WID), BF),
+                pltpu.VMEM((3, rw, WID), F32),
+                pltpu.SemaphoreType.DMA((3,)),
+                pltpu.SemaphoreType.DMA((5,)),
+            ],
             compiler_params=pltpu.CompilerParams(vmem_limit_bytes=58 * 1024 * 1024),
         )(first_in, grad_second, weights)
 

time: 82.3 us -> 73.5 us (0.89)
  the two profiles are of different devices: /device:TPU:1 before, /device:TPU:8 now
where the time goes in v3:
time: 73.5 us; the launch traced here: 73.4 us
  Pallas kernels  72.7 us (99%)
    pallas_call x1, Pallas kernels, shards(): pl.pallas_call(functools.partial(kernel, nz, ny, 1.0 / total_rows ** 0.5)...  71 us
    pallas_call x1, Pallas kernels, shards(): pl.pallas_call(hand_out, out_shape=(stream, stream, grads, grads, grads),...  1.7 us

profile of v3, /device:TPU:8, one launch (start us, length us, event | category | flops | bytes accessed | tf_op | source)
XLA Modules:
  0.0 73.4 jit_solution(16172664766894738801)
XLA Ops:
  0.6 71.0 %shard_map.128 = (bf16[1,256,256]{2,1,0:T(8,128)(2,1)}, bf16[1,256,256]{2,1,0:T(8,128)(2,1)}, f32[3,8,256]{2,1,0:T(8,128)}) custom-call(bf16[1,256,256]{2,1,0:T(8,128)(2,1)} %pt_h.1, bf16[1,256,256]{2,1,0:T(8,128)(2,1)} %mo_h.1, bf16[1,256,256]{2,1,0:T(8,128)(2,1)} %gm_h.1, bf16[1,256,256]{2,1,0:T(8,128)(2,1)} %gp_h.1, bf16[1024,256]{1,0:T(8,128)(2,1)} %wq_h.1, ...), custom_call_target="tpu_custom_call" | custom-call | flops 1800000000 | bytes 4000000 | tf_op jit(solution)/shard_map/pallas_call | solution.py:584
  71.7 1.7 %shard_map.129 = (bf16[1,256,256]{2,1,0:T(8,128)(2,1)}, bf16[1,256,256]{2,1,0:T(8,128)(2,1)}, f32[8,256]{1,0:T(8,128)}, f32[8,256]{1,0:T(8,128)}, f32[8,256]{1,0:T(8,128)}) custom-call(bf16[1,256,256]{2,1,0:T(8,128)(2,1)} %get-tuple-element.8.fi, bf16[1,256,256]{2,1,0:T(8,128)(2,1)} %get-tuple-element.9.gs, f32[3,8,256]{2,1,0:T(8,128)} %get-tuple-element.10.wg), custom_call_target="tpu_custom_call" | custom-call | tf_op jit(solution)/shard_map/pallas_call | solution.py:640

commit v4 on v3

--- a/solution.py
+++ b/solution.py
@@ -101,6 +101,7 @@
     osem,
     ssem,
     rsem,
+    know,
 ):
     seq = lax.axis_index("seq")
     x = lax.axis_index("head")
@@ -128,7 +129,7 @@
     barrier = pltpu.get_barrier_semaphore()
     peers = [at_x(lax.rem(x + d, NX)) for d in range(1, NX)]
     peers += [sibling]
-    peers += [at_z(d) for d in range(1, nz)]
+    peers += [at_z(d) for d in (1, nz - 1, 2, nz - 2)]
     peers += [at_y(lax.rem(y + d, ny)) for d in range(1, ny)]
     for peer in peers:
         pl.semaphore_signal(barrier, inc=1, device_id=peer, device_id_type=MESH)
@@ -187,6 +188,8 @@
     for name, copy in local.items():
         if name not in early:
             copy.start()
+    for i, step in enumerate((2, -2)):
+        pl.semaphore_signal(know.at[i], inc=1, device_id=at_z(step), device_id_type=MESH)
     c_gm = send(gm_h.at[0, :, others], gmh.at[c], sibling)
     c_mo = send(mo_h.at[0, :, others], moh.at[c], sibling)
 
@@ -317,6 +320,11 @@
 
     forward = Scan(1, fmsg, fgot, ftwo, fst)
     forward.begin(outer_sum(fk, vb, chip_last))
+    for i in range(2):
+        pl.semaphore_wait(know.at[i], 1)
+    if nz > 4:
+        for i, step in enumerate((4, -4)):
+            pl.semaphore_signal(know.at[2 + i], inc=1, device_id=at_z(step), device_id_type=MESH)
 
     local["wq"].wait()
     for b in range(2):
@@ -476,6 +484,9 @@
         dfeat = dfk[b] + nt(masked, bst[...])
         dh[1, b * TOK : (b + 1) * TOK, mine] = feature_grad(dfeat, fk[b], kb[b])
     c_dk = send(dh.at[1, :, mine], dh.at[1, :, mine], sibling)
+    if nz > 4:
+        for i in range(2):
+            pl.semaphore_wait(know.at[2 + i], 1)
     z_q = z_send(0, ring_q.total(own_q))
     local["w0"].wait()
     local["w1"].wait()
@@ -631,6 +642,7 @@
                 pltpu.SemaphoreType.DMA((4,)),
                 pltpu.SemaphoreType.DMA((copies,)),
                 pltpu.SemaphoreType.DMA((copies,)),
+                pltpu.SemaphoreType.REGULAR((4,)),
             ],
             compiler_params=limit,
             cost_estimate=pl.CostEstimate(

time: 73.5 us -> 71.2 us (0.969)
  the two profiles are of different devices: /device:TPU:8 before, /device:TPU:1 now
where the time goes in v4:
time: 71.2 us; the launch traced here: 71.1 us
  Pallas kernels  70.4 us (99%)
    pallas_call x1, Pallas kernels, shards(): pl.pallas_call(functools.partial(kernel, nz, ny, 1.0 / total_rows ** 0.5)...  68.7 us
    pallas_call x1, Pallas kernels, shards(): pl.pallas_call(hand_out, out_shape=(stream, stream, grads, grads, grads),...  1.7 us

profile of v4, /device:TPU:1, one launch (start us, length us, event | category | flops | bytes accessed | tf_op | source)
XLA Modules:
  0.0 71.1 jit_solution(17851827991442162403)
XLA Ops:
  0.6 68.7 %shard_map.128 = (bf16[1,256,256]{2,1,0:T(8,128)(2,1)}, bf16[1,256,256]{2,1,0:T(8,128)(2,1)}, f32[3,8,256]{2,1,0:T(8,128)}) custom-call(bf16[1,256,256]{2,1,0:T(8,128)(2,1)} %pt_h.1, bf16[1,256,256]{2,1,0:T(8,128)(2,1)} %mo_h.1, bf16[1,256,256]{2,1,0:T(8,128)(2,1)} %gm_h.1, bf16[1,256,256]{2,1,0:T(8,128)(2,1)} %gp_h.1, bf16[1024,256]{1,0:T(8,128)(2,1)} %wq_h.1, ...), custom_call_target="tpu_custom_call" | custom-call | flops 1800000000 | bytes 4000000 | tf_op jit(solution)/shard_map/pallas_call | solution.py:595
  69.4 1.7 %shard_map.129 = (bf16[1,256,256]{2,1,0:T(8,128)(2,1)}, bf16[1,256,256]{2,1,0:T(8,128)(2,1)}, f32[8,256]{1,0:T(8,128)}, f32[8,256]{1,0:T(8,128)}, f32[8,256]{1,0:T(8,128)}) custom-call(bf16[1,256,256]{2,1,0:T(8,128)(2,1)} %get-tuple-element.8.fi, bf16[1,256,256]{2,1,0:T(8,128)(2,1)} %get-tuple-element.9.gs, f32[3,8,256]{2,1,0:T(8,128)} %get-tuple-element.10.wg), custom_call_target="tpu_custom_call" | custom-call | tf_op jit(solution)/shard_map/pallas_call | solution.py:652
